TPU v7x, 512 devices: a whole 4x4x16 slice. The times are simulated.
512 devices in a mesh: dp: 32 (over z, core), tensor: 16 (over y, x).
Axes of the slice: x: 4, y: 4, z: 16, core: 2. Of those that a mesh axis runs over, the one named last changes fastest.
Arguments:
- hidden: bfloat16 [8192, 4096], P(('dp', 'tensor')), may hold values from -3.6 to 3.6
- lengths: int32 [32, 32], P('dp'), may hold values from 1 to 80, 256 in all within a row
- positives: int32 [256], replicated, may hold values from 0 to 767, as said below
- negatives: int32 [256, 7], replicated, may hold values from 1 to 766, as said below
- in_gain: float32 [4096], replicated, may hold values from 0.25 to 1.75
- wq: bfloat16 [4096, 2048], P(None, 'tensor'), may hold values from -0.09375 to 0.09375
- wkv: bfloat16 [4096, 2048], P(None, 'tensor'), may hold values from -0.09375 to 0.09375
- q_gain: float32 [128], replicated, may hold values from 0.25 to 1.75
- k_gain: float32 [128], replicated, may hold values from 0.25 to 1.75
- wo: bfloat16 [2048, 4096], P('tensor'), may hold values from -0.125 to 0.125
- out_gain: float32 [4096], replicated, may hold values from 0.25 to 1.75
Outputs:
- d_hidden: bfloat16 [8192, 4096], P(('dp', 'tensor'))
- loss: float32 [], replicated
Inputs may be any that keep to these rules, and one draw needn't show every extreme that they name: Each group's 32 lengths sum to 256, and one of them is exactly 80. The 256 positives are distinct passages. The 7 hard negatives of a query are distinct, and none of them is any query's positive.
All inputs are finite; a program needn't handle non-finite values.
Results may differ from a plain program's by a relative error of at most 0.023.
Values may be sent and summed in bfloat16 or wider, within the bound.
No kernel may reach another device: no remote copies, remote signals or barrier semaphores. Data moves between devices by JAX's collectives and lax.ppermute only.
A program may use at most 64 MiB of HBM per device.

v0:
```python
import math
import jax
import jax.numpy as jnp
from jax import lax
from jax.sharding import PartitionSpec as P

QDEV = 8
EPSILON = 1e-06
SOFTMAX_TEMPER = 0.05
LOSS_MULTIPLIER = 8192.0
ROPE_BASE = 1000000.0


def swapped(value, axis, apart):
    mask = 2**apart
    pairs = [(source, source ^ mask) for source in range(lax.axis_size(axis))]
    return lax.ppermute(value, axis, pairs)


def rms_scale(tensor):
    return lax.rsqrt(jnp.mean(tensor * tensor, axis=-1, keepdims=True) + EPSILON)


def rope_tables(position, head_width):
    halfway = head_width // 2
    frequency = ROPE_BASE ** (-(jnp.arange(halfway, dtype=jnp.float32) * (2.0 / head_width)))
    angles = position[:, None] * frequency[None, :]
    angles = jnp.concatenate([angles, angles], axis=-1)
    return (jnp.cos(angles), jnp.sin(angles))


def rotate(tensor, cosine, sine):
    halfway = tensor.shape[-1] // 2
    turned = jnp.concatenate([-tensor[..., halfway:], tensor[..., :halfway]], axis=-1)
    return tensor * cosine + turned * sine


def segment_layout(lengths_row, total_tokens):
    seq_ends = jnp.cumsum(lengths_row)
    starts = seq_ends - lengths_row
    token_index = jnp.arange(total_tokens, dtype=jnp.int32)
    inside = (token_index[:, None] >= starts[None, :]) & (token_index[:, None] < seq_ends[None, :])
    offset = jnp.sum(jnp.where(inside, starts[None, :], 0), axis=1)
    position = (token_index - offset).astype(jnp.float32)
    return (inside, position, seq_ends - 1)


def head_forward(raw, gain, cosine, sine):
    inverse = rms_scale(raw)
    unit_form = raw * inverse
    return (unit_form, inverse, rotate(unit_form * gain, cosine, sine))


def norm_backward(grad, unit_form, inverse, gain):
    scaled = grad * gain
    return inverse * (scaled - unit_form * jnp.mean(unit_form * scaled, axis=-1, keepdims=True))


def head_backward(grad_rot, unit_form, inverse, gain, cosine, sine):
    return norm_backward(rotate(grad_rot, cosine, -sine), unit_form, inverse, gain)


def contrast(embeds16, positives, negatives):
    groups = embeds16.shape[0]
    feature_count = embeds16.shape[2]
    query_rows = embeds16[:, :QDEV].reshape(groups * QDEV, feature_count)
    passage_rows = embeds16[:, QDEV:].reshape(-1, feature_count)
    query_total_count = query_rows.shape[0]
    passage_ids = jnp.arange(passage_rows.shape[0], dtype=jnp.int32)
    similarity_logits = (
        jnp.dot(query_rows, passage_rows.T, preferred_element_type=jnp.float32) / SOFTMAX_TEMPER
    )
    positive_hot = positives[:, None] == passage_ids[None, :]
    hard_hot = jnp.any(negatives[:, :, None] == passage_ids[None, None, :], axis=1)
    permitted_mask = jnp.any(positive_hot, axis=0)[None, :] | hard_hot
    weight_params = jnp.where(
        permitted_mask, jnp.exp(similarity_logits - 1.0 / SOFTMAX_TEMPER), 0.0
    )
    running_totals = jnp.sum(weight_params, axis=1, keepdims=True)
    target_labels = jnp.sum(jnp.where(positive_hot, similarity_logits, 0.0), axis=1)
    loss = jnp.mean(jnp.log(running_totals[:, 0]) + 1.0 / SOFTMAX_TEMPER - target_labels)
    scaling_factor = LOSS_MULTIPLIER / (query_total_count * SOFTMAX_TEMPER)
    coef16 = (
        scaling_factor * (weight_params / running_totals - positive_hot.astype(jnp.float32))
    ).astype(jnp.bfloat16)
    d_queries = jnp.dot(coef16, passage_rows, preferred_element_type=jnp.float32)
    d_passages = jnp.dot(coef16.T, query_rows, preferred_element_type=jnp.float32)
    joined = jnp.concatenate(
        [
            d_queries.reshape(groups, QDEV, feature_count),
            d_passages.reshape(groups, -1, feature_count),
        ],
        axis=1,
    )
    return (loss, joined)


def on_device(
    hidden, lengths, positives, negatives, in_gain, wq, wkv, q_gain, k_gain, wo, out_gain
):
    tensor_count = lax.axis_size("tensor")
    own_rows = hidden.shape[0]
    tokens_count = own_rows * tensor_count
    head_width = wq.shape[1]
    root = math.sqrt(head_width)
    is_even = lax.axis_index("tensor") % 2 == 0
    own_index = lax.axis_index("tensor") * own_rows + jnp.arange(own_rows, dtype=jnp.int32)
    inside, position, last = segment_layout(lengths[0], tokens_count)
    hidden32 = hidden.astype(jnp.float32)
    inverse_in = rms_scale(hidden32)
    normed = (hidden32 * inverse_in * in_gain).astype(jnp.bfloat16)
    partner = swapped(wkv, "tensor", 0)
    both = jnp.concatenate(
        [jnp.where(is_even, wkv, partner), jnp.where(is_even, partner, wkv)], axis=1
    )
    piece = lax.all_gather(normed, "tensor", axis=0, tiled=True)
    kv_raw = jnp.dot(piece, both, preferred_element_type=jnp.float32)
    key_raw = kv_raw[:, :head_width]
    value_raw = kv_raw[:, head_width:]
    value16 = value_raw.astype(jnp.bfloat16)
    cos_key, sin_key = rope_tables(position, head_width)
    key_unit, key_inverse, key_rot = head_forward(key_raw, k_gain, cos_key, sin_key)
    key16 = key_rot.astype(jnp.bfloat16)
    last_rows = jnp.take(piece, last, axis=0)
    query_raw = jnp.dot(last_rows, wq, preferred_element_type=jnp.float32)
    cos_query, sin_query = rope_tables(jnp.take(position, last), head_width)
    query_unit, query_inverse, query_rot = head_forward(query_raw, q_gain, cos_query, sin_query)
    query16 = query_rot.astype(jnp.bfloat16)
    shift = root * jnp.max(q_gain) * jnp.max(k_gain)
    scores = jnp.dot(query16, key16.T, preferred_element_type=jnp.float32) / root
    weight_params = jnp.where(inside.T, jnp.exp(scores - shift), 0.0)
    probs = weight_params / jnp.sum(weight_params, axis=-1, keepdims=True)
    probs16 = probs.astype(jnp.bfloat16)
    attn16 = jnp.dot(probs16, value16, preferred_element_type=jnp.float32).astype(jnp.bfloat16)
    own_last = (last[:, None] == own_index[None, :]).astype(jnp.float32)
    partial_rows = jnp.dot(attn16, wo, preferred_element_type=jnp.float32)
    partial_rows = partial_rows + jnp.dot(own_last, hidden32, precision=lax.Precision.HIGHEST)
    resid = lax.psum(partial_rows, "tensor")
    resid_inverse = rms_scale(resid)
    resid_unit = resid * resid_inverse
    final = resid_unit * out_gain
    final_inverse = lax.rsqrt(jnp.sum(final * final, axis=-1, keepdims=True) + EPSILON)
    embed = final * final_inverse
    everyone = lax.all_gather(embed.astype(jnp.bfloat16), "dp", axis=0, tiled=True)
    groups = lax.axis_size("dp")
    loss, d_every = contrast(everyone.reshape(groups, -1, everyone.shape[1]), positives, negatives)
    d_embed = lax.dynamic_index_in_dim(d_every, lax.axis_index("dp"), 0, keepdims=False)
    d_final = final_inverse * (d_embed - embed * jnp.sum(embed * d_embed, axis=-1, keepdims=True))
    d_resid = norm_backward(d_final, resid_unit, resid_inverse, out_gain)
    d_attn16 = jnp.dot(
        d_resid.astype(jnp.bfloat16), wo.T, preferred_element_type=jnp.float32
    ).astype(jnp.bfloat16)
    d_probs = jnp.dot(d_attn16, value16.T, preferred_element_type=jnp.float32)
    d_scores16 = (
        probs * (d_probs - jnp.sum(probs * d_probs, axis=-1, keepdims=True)) / root
    ).astype(jnp.bfloat16)
    d_query_rot = jnp.dot(d_scores16, key16, preferred_element_type=jnp.float32)
    d_key_rot = jnp.dot(d_scores16.T, query16, preferred_element_type=jnp.float32)
    d_value = jnp.dot(probs16.T, d_attn16, preferred_element_type=jnp.float32)
    d_key_raw = head_backward(d_key_rot, key_unit, key_inverse, k_gain, cos_key, sin_key)
    d_query_raw = head_backward(
        d_query_rot, query_unit, query_inverse, q_gain, cos_query, sin_query
    )
    mine = jnp.where(is_even, d_key_raw, d_value)
    theirs = jnp.where(is_even, d_value, d_key_raw)
    column16 = (mine + swapped(theirs, "tensor", 0)).astype(jnp.bfloat16)
    query_term = jnp.dot(d_query_raw.astype(jnp.bfloat16), wq.T, preferred_element_type=jnp.float32)
    row_index = jnp.arange(own_rows * lax.axis_size("tensor"), dtype=jnp.int32)
    chosen = (row_index[:, None] == last[None, :]).astype(jnp.float32)
    product = jnp.dot(column16, wkv.T, preferred_element_type=jnp.float32)
    d_normed = lax.psum_scatter(
        (product + jnp.dot(chosen, query_term, precision=lax.Precision.HIGHEST)).astype(
            jnp.bfloat16
        ),
        "tensor",
        scatter_dimension=0,
        tiled=True,
    ).astype(jnp.float32)
    d_hidden = norm_backward(d_normed, hidden32 * inverse_in, inverse_in, in_gain)
    d_hidden = d_hidden + jnp.dot(own_last.T, d_resid, precision=lax.Precision.HIGHEST)
    return (d_hidden.astype(jnp.bfloat16), loss)


def solution(mesh):
    placed = (
        P(("dp", "tensor"), None),
        P("dp", None),
        P(),
        P(),
        P(),
        P(None, "tensor"),
        P(None, "tensor"),
        P(),
        P(),
        P("tensor", None),
        P(),
    )
    return jax.shard_map(
        on_device,
        mesh=mesh,
        in_specs=placed,
        out_specs=(P(("dp", "tensor"), None), P()),
        check_vma=False,
    )
```

profile of v0, /device:TPU:32, one launch (start us, length us, event | category | flops | bytes accessed | tf_op | source)
XLA Modules:
  0.0 409.4 jit_solution(15315074954518132723)
XLA Ops:
  7.2 1.1 fusion.41
  8.4 1.7 fusion.37
  10.1 3.4 collective-permute-start
  13.5 0.7 copy.23
  14.4 0.7 fusion.86
  15.2 1.3 reduce_max.19
  16.5 1.3 reduce_max.18
  19.0 0.7 gather_fusion.1
  19.9 1.2 fusion.66
  21.1 16.7 %collective-permute-done = bf16[4096,128]{1,0:T(8,128)(2,1)S(1)} collective-permute-done((bf16[4096,128]{1,0:T(8,128)(2,1)}, bf16[4096,128]{1,0:T(8,128)(2,1)S(1)}, u32[]{:S(2)}, u32[]{:S(2)}) %collective-permute-start) | collective-permute-done | bytes 1048608 | tf_op jit(solution)/shard_map/ppermute | solution.py:17
  37.8 2.7 broadcast_select_fusion.1
  40.5 35.5 %all-gather.3.cloned.1.call-done = bf16[256,4096]{1,0:T(8,128)(2,1)} async-done(((bf16[16,4096]{1,0:T(8,128)(2,1)}), bf16[256,4096]{1,0:T(8,128)(2,1)}) %all-gather.3.cloned.1.call-update) | async-done | bytes 2097168 | tf_op jit(solution)/shard_map/all_gather | solution.py:116
  76.0 2.8 gather_fusion
  79.5 3.1 fusion.3
  83.7 1.3 convolution_add_fusion.1
  85.0 115.5 %all-reduce.2.cloned.1.call-done = f32[32,4096]{1,0:T(8,128)} async-done(((f32[32,4096]{1,0:T(8,128)}), f32[32,4096]{1,0:T(8,128)}) %all-reduce.2.cloned.1.call-update) | async-done | bytes 524304 | tf_op jit(solution)/shard_map/psum | solution.py:138
  200.5 1.2 multiply_reduce_fusion.2
  201.7 1.3 multiply_reduce_fusion.1
  203.0 1.9 fusion.33
  205.4 0.9 fusion
  206.3 77.7 %all-gather.5.cloned.1.call-done = bf16[1024,4096]{1,0:T(8,128)(2,1)} async-done(((bf16[32,4096]{1,0:T(8,128)(2,1)}), bf16[1024,4096]{1,0:T(8,128)(2,1)}) %all-gather.5.cloned.1.call-update) | async-done | bytes 8388624 | tf_op jit(solution)/shard_map/all_gather | solution.py:144
  284.0 3.2 slice.60
  287.2 3.7 select_reduce_fusion
  291.3 4.1 %fusion.29 = f32[32,8,4096]{2,1,0:T(8,128)} fusion(bf16[768,4096,1]{1,0,2:T(8,128)(2,1)S(1)} %bitcast.69, s32[256]{0:T(256)S(1)} %copy-done.11, f32[256,768]{1,0:T(8,128)S(1)} %get-tuple-element.28, pred[256,768]{1,0:T(8,128)(4,1)S(1)} %fusion, f32[256]{0:T(256)S(1)} %get-tuple-element.3, pred[768]{0:T(1024)(128)(4,1)S(1)} %fusion.21), kind=kOutput, calls=%fused_computation.53 | convolution fusion | flops 1612382208 | bytes 11471616 | tf_op jit(solution)/shard_map/dot_general | solution.py:86
  295.6 3.5 fusion.7
  302.4 3.6 collective-permute-start.1
  306.5 1.8 fusion.58
  308.3 1.6 collective-permute-done.1
  309.9 2.1 fusion.1
  313.3 85.2 %reduce-scatter.2.cloned.1.call-done = bf16[16,4096]{1,0:T(8,128)(2,1)} async-done(((bf16[256,4096]{1,0:T(8,128)(2,1)}), bf16[16,4096]{1,0:T(8,128)(2,1)}) %reduce-scatter.2.cloned.1.call-update) | async-done | bytes 131088 | tf_op jit(solution)/shard_map/reduce_scatter | solution.py:171
  398.6 1.1 fusion.38
  399.7 2.0 fusion.2
  (79 shorter events, 7.5 us)
Async XLA Ops:
  7.2 71.7 %copy-start = (bf16[4096,128]{1,0:T(8,128)(2,1)S(1)}, bf16[4096,128]{1,0:T(8,128)(2,1)}, u32[]{:S(2)}) copy-start(bf16[4096,128]{1,0:T(8,128)(2,1)} %param.16) | copy-start | bytes 3145732
  7.2 68.8 %all-gather.3.cloned.1.call-start = ((), (), s32[]{:S(2)}) async-start(), calls=%async_computation.1 | async-start | bytes 2228224 | tf_op jit(solution)/shard_map/all_gather | solution.py:116
  10.1 190.5 %all-reduce.2.cloned.1.call-start = ((), (), s32[]{:S(2)}) async-start(), calls=%async_computation.2 | async-start | bytes 1048576 | tf_op jit(solution)/shard_map/psum | solution.py:138
  10.1 27.7 %collective-permute-start = (bf16[4096,128]{1,0:T(8,128)(2,1)}, bf16[4096,128]{1,0:T(8,128)(2,1)S(1)}, u32[]{:S(2)}, u32[]{:S(2)}) collective-permute-start(bf16[4096,128]{1,0:T(8,128)(2,1)} %param.17), channel_id=1, source_target_pairs={{0,1},{1,0},{2,3},{3,2},{4,5},{5,4},{6,7},{7,6},{8,9},{9,8},{10,11... | collective-permute-start | bytes 3145736 | tf_op jit(solution)/shard_map/ppermute | solution.py:17
  19.9 59.4 %copy-start.9 = (f32[128]{0:T(128)S(1)}, f32[128]{0:T(128)}, u32[]{:S(2)}) copy-start(f32[128]{0:T(128)} %param.18) | copy-start | bytes 1540
  78.8 3.8 copy-start.10
  78.9 4.8 %copy-start.3 = (bf16[128,4096]{1,0:T(8,128)(2,1)S(1)}, bf16[128,4096]{1,0:T(8,128)(2,1)}, u32[]{:S(2)}) copy-start(bf16[128,4096]{1,0:T(8,128)(2,1)} %param.20) | copy-start | bytes 3145732
  79.5 122.2 %copy-start.6 = (f32[4096]{0:T(1024)S(1)}, f32[4096]{0:T(1024)}, u32[]{:S(2)}) copy-start(f32[4096]{0:T(1024)} %param.21) | copy-start | bytes 49156
  82.6 122.6 %copy-start.11 = (s32[256]{0:T(256)S(1)}, s32[256]{0:T(256)}, u32[]{:S(2)}) copy-start(s32[256]{0:T(256)} %param.13) | copy-start | bytes 3076
  82.6 122.7 %copy-start.8 = (s32[256,7]{0,1:T(8,128)S(1)}, s32[256,7]{0,1:T(8,128)}, u32[]{:S(2)}) copy-start(s32[256,7]{0,1:T(8,128)} %param.14) | copy-start | bytes 21508
  85.0 199.0 %all-gather.5.cloned.1.call-start = ((), (), s32[]{:S(2)}) async-start(), calls=%async_computation.3 | async-start | bytes 8650752 | tf_op jit(solution)/shard_map/all_gather | solution.py:144
  204.9 193.6 %reduce-scatter.2.cloned.1.call-start = ((), (), s32[]{:S(2)}) async-start(), calls=%async_computation.4 | async-start | bytes 2228224 | tf_op jit(solution)/shard_map/reduce_scatter | solution.py:171
  295.6 3.6 copy-start.1
  295.6 3.6 copy-start.4
  300.5 9.4 %copy-start.2 = (bf16[4096,128]{1,0:T(8,128)(2,1)S(1)}, bf16[4096,128]{1,0:T(8,128)(2,1)}, u32[]{:S(2)}) copy-start(bf16[4096,128]{1,0:T(8,128)(2,1)} %param.17) | copy-start | bytes 3145732
  302.4 7.5 %collective-permute-start.1 = (f32[256,128]{0,1:T(8,128)S(1)}, f32[256,128]{0,1:T(8,128)S(1)}, u32[]{:S(2)}, u32[]{:S(2)}) collective-permute-start(f32[256,128]{0,1:T(8,128)S(1)} %get-tuple-element.31), channel_id=1, source_target_pairs={{0,1},{1,0},{2,3},{3,2},{4,5},{5,4},{6,7},{7,6},{8,9},{9,8},{10,11... | collective-permute-start | bytes 393224 | tf_op jit(solution)/shard_map/ppermute | solution.py:17
  309.9 88.7 %copy-start.5 = (bf16[16,4096]{1,0:T(8,128)(2,1)S(1)}, bf16[16,4096]{1,0:T(8,128)(2,1)}, u32[]{:S(2)}) copy-start(bf16[16,4096]{1,0:T(8,128)(2,1)} %param.11) | copy-start | bytes 393220
  309.9 88.7 %copy-start.7 = (f32[4096]{0:T(1024)S(1)}, f32[4096]{0:T(1024)}, u32[]{:S(2)}) copy-start(f32[4096]{0:T(1024)} %param.15) | copy-start | bytes 49156
Sparse Core Ops, SparseCore 0:
  11.6 64.3 all-gather.2
  85.1 115.3 all-reduce.1
  205.1 78.8 all-gather.4
  312.2 86.3 reduce-scatter.1
where the time goes:
time: 410 us; the launch traced here: 409 us
  waiting for transfers between devices  332 us (81%)
  matrix products  25.3 us (6%)
  other arithmetic  19.4 us (5%)
  between operations  17.2 us (4%)
  local copies, waits for them, and re-layouts  7.71 us (2%)
  starting transfers between devices  7.35 us (2%)
    psum x1, waiting for transfers between devices, on_device(): resid = lax.psum(partial_rows, 'tensor')  115 us
    reduce_scatter x1, waiting for transfers between devices, on_device(): lax.psum_scatter((product + jnp.dot(chosen, query_term, precision=lax.Pre...  85.2 us
    all_gather x1, waiting for transfers between devices, on_device(): lax.all_gather(embed.astype(jnp.bfloat16), 'dp', axis=0, tiled=True)  77.7 us
    all_gather x1, waiting for transfers between devices, on_device(): piece = lax.all_gather(normed, 'tensor', axis=0, tiled=True)  35.5 us
    ppermute x2, waiting for transfers between devices, swapped(): return lax.ppermute(value, axis, pairs)  18.3 us
  transfers between devices with their start and end apart: 6, of which 6 were waited for; matrix products, arithmetic and copies ran while one was open for 3% of the time, Pallas kernels for 0%

commit v1 on v0

--- a/solution.py
+++ b/solution.py
@@ -135,7 +135,9 @@
     own_last = (last[:, None] == own_index[None, :]).astype(jnp.float32)
     partial_rows = jnp.dot(attn16, wo, preferred_element_type=jnp.float32)
     partial_rows = partial_rows + jnp.dot(own_last, hidden32, precision=lax.Precision.HIGHEST)
-    resid = lax.psum(partial_rows, "tensor")
+    resid = partial_rows
+    for hop in (1, 2, 4, 8):
+        resid = resid + lax.ppermute(resid, "tensor", [(dev, dev ^ hop) for dev in range(16)])
     resid_inverse = rms_scale(resid)
     resid_unit = resid * resid_inverse
     final = resid_unit * out_gain

time: 410 us -> 352 us (0.86)
  waiting for transfers between devices: 332 us -> 257 us
  starting transfers between devices: 7.35 us -> 21.5 us
    psum x1 -> x0, waiting for transfers between devices: 115 us -> none  [on_device(): resid = lax.psum(partial_rows, 'tensor')]
    ppermute x0 -> x4, waiting for transfers between devices: none -> 42.2 us  [on_device(): lax.ppermute(resid, 'tensor', [(dev, dev ^ hop) for dev in range(16)])]
    ppermute x0 -> x4, starting transfers between devices: none -> 14.1 us  [on_device(): lax.ppermute(resid, 'tensor', [(dev, dev ^ hop) for dev in range(16)])]
  transfers between devices with their start and end apart: 6 -> 9, of which waited for: 6 -> 9; matrix products, arithmetic and copies ran while one was open for 3% -> 4% of each run, Pallas kernels for 0% -> 0%
where the time goes in v1:
time: 352 us; the launch traced here: 351 us
  waiting for transfers between devices  257 us (73%)
  matrix products  26.2 us (7%)
  starting transfers between devices  21.5 us (6%)
  other arithmetic  19.3 us (5%)
  between operations  17.4 us (5%)
  local copies, waits for them, and re-layouts  9.33 us (3%)
    reduce_scatter x1, waiting for transfers between devices, on_device(): lax.psum_scatter((product + jnp.dot(chosen, query_term, precision=lax.Pre...  85.3 us
    all_gather x1, waiting for transfers between devices, on_device(): lax.all_gather(embed.astype(jnp.bfloat16), 'dp', axis=0, tiled=True)  76.4 us
    ppermute x4, waiting for transfers between devices, on_device(): lax.ppermute(resid, 'tensor', [(dev, dev ^ hop) for dev in range(16)])  42.2 us
    all_gather x1, waiting for transfers between devices, on_device(): piece = lax.all_gather(normed, 'tensor', axis=0, tiled=True)  35 us
    ppermute x2, waiting for transfers between devices, swapped(): return lax.ppermute(value, axis, pairs)  18.3 us
    ppermute x4, starting transfers between devices, on_device(): lax.ppermute(resid, 'tensor', [(dev, dev ^ hop) for dev in range(16)])  14.1 us
  transfers between devices with their start and end apart: 9, of which 9 were waited for; matrix products, arithmetic and copies ran while one was open for 4% of the time, Pallas kernels for 0%

profile of v1, /device:TPU:32, one launch (start us, length us, event | category | flops | bytes accessed | tf_op | source)
XLA Modules:
  0.0 351.0 jit_solution(16967846367608064676)
XLA Ops:
  8.9 1.7 fusion.37
  10.6 3.4 collective-permute-start
  15.8 1.3 reduce_max.19
  17.0 1.3 reduce_max.18
  20.4 1.2 fusion.66
  21.6 16.7 %collective-permute-done = bf16[4096,128]{1,0:T(8,128)(2,1)S(1)} collective-permute-done((bf16[4096,128]{1,0:T(8,128)(2,1)}, bf16[4096,128]{1,0:T(8,128)(2,1)S(1)}, u32[]{:S(2)}, u32[]{:S(2)}) %collective-permute-start) | collective-permute-done | bytes 1048608 | tf_op jit(solution)/shard_map/ppermute | solution.py:17
  38.3 2.7 broadcast_select_fusion.1
  41.0 35.0 %all-gather.3.cloned.1.call-done = bf16[256,4096]{1,0:T(8,128)(2,1)} async-done(((bf16[16,4096]{1,0:T(8,128)(2,1)}), bf16[256,4096]{1,0:T(8,128)(2,1)}) %all-gather.3.cloned.1.call-update) | async-done | bytes 2097168 | tf_op jit(solution)/shard_map/all_gather | solution.py:116
  76.0 2.8 gather_fusion
  79.5 3.1 fusion.3
  85.4 3.1 collective-permute-start.1
  88.5 11.7 %collective-permute-done.1 = f32[32,4096]{1,0:T(8,128)S(1)} collective-permute-done((f32[32,4096]{1,0:T(8,128)S(1)}, f32[32,4096]{1,0:T(8,128)S(1)}, u32[]{:S(2)}, u32[]{:S(2)}) %collective-permute-start.1) | collective-permute-done | bytes 524320 | tf_op jit(solution)/shard_map/ppermute | solution.py:140
  100.2 4.0 %collective-permute-start.2 = (f32[32,4096]{1,0:T(8,128)S(1)}, f32[32,4096]{1,0:T(8,128)S(1)}, u32[]{:S(2)}, u32[]{:S(2)}) collective-permute-start(f32[32,4096]{1,0:T(8,128)S(1)} %add.174), channel_id=1, source_target_pairs={{0,2},{1,3},{2,0},{3,1},{4,6},{5,7},{6,4},{7,5},{8,10},{9,11},{10,... | collective-permute-start | bytes 1572872 | tf_op jit(solution)/shard_map/ppermute | solution.py:140
  104.2 11.3 %collective-permute-done.2 = f32[32,4096]{1,0:T(8,128)S(1)} collective-permute-done((f32[32,4096]{1,0:T(8,128)S(1)}, f32[32,4096]{1,0:T(8,128)S(1)}, u32[]{:S(2)}, u32[]{:S(2)}) %collective-permute-start.2) | collective-permute-done | bytes 524320 | tf_op jit(solution)/shard_map/ppermute | solution.py:140
  115.6 3.1 collective-permute-start.3
  118.6 9.8 %collective-permute-done.3 = f32[32,4096]{1,0:T(8,128)S(1)} collective-permute-done((f32[32,4096]{1,0:T(8,128)S(1)}, f32[32,4096]{1,0:T(8,128)S(1)}, u32[]{:S(2)}, u32[]{:S(2)}) %collective-permute-start.3) | collective-permute-done | bytes 524320 | tf_op jit(solution)/shard_map/ppermute | solution.py:140
  128.5 4.0 %collective-permute-start.4 = (f32[32,4096]{1,0:T(8,128)S(1)}, f32[32,4096]{1,0:T(8,128)S(1)}, u32[]{:S(2)}, u32[]{:S(2)}) collective-permute-start(f32[32,4096]{1,0:T(8,128)S(1)} %add.176), channel_id=1, source_target_pairs={{0,8},{1,9},{2,10},{3,11},{4,12},{5,13},{6,14},{7,15},{8,0},{9,1},... | collective-permute-start | bytes 1572872 | tf_op jit(solution)/shard_map/ppermute | solution.py:140
  132.5 9.4 %collective-permute-done.4 = f32[32,4096]{1,0:T(8,128)S(1)} collective-permute-done((f32[32,4096]{1,0:T(8,128)S(1)}, f32[32,4096]{1,0:T(8,128)S(1)}, u32[]{:S(2)}, u32[]{:S(2)}) %collective-permute-start.4) | collective-permute-done | bytes 524320 | tf_op jit(solution)/shard_map/ppermute | solution.py:140
  144.4 1.6 fusion
  146.0 76.4 %all-gather.5.cloned.1.call-done = bf16[1024,4096]{1,0:T(8,128)(2,1)} async-done(((bf16[32,4096]{1,0:T(8,128)(2,1)}), bf16[1024,4096]{1,0:T(8,128)(2,1)}) %all-gather.5.cloned.1.call-update) | async-done | bytes 8388624 | tf_op jit(solution)/shard_map/all_gather | solution.py:146
  222.4 3.2 slice.60
  225.6 4.3 %select_reduce_fusion = (f32[256]{0:T(256)}, f32[256]{0:T(256)S(1)}, f32[256,768]{1,0:T(8,128)S(1)}) fusion(s32[256]{0:T(256)S(1)} %copy-done.27, pred[256,768]{1,0:T(8,128)(4,1)S(1)} %fusion, pred[768]{0:T(1024)(128)(4,1)S(1)} %fusion.21, bf16[768,4096]{1,0:T(8,128)(2,1)S(1)} %bitcast.68, bf16[32,32,4096]{2,1,0:T(8,128)(2,1)} %bitcast.66), kind=kOutput, calls=%fused_computation.33 | convolution fusion | flops 1612185088 | bytes 9375488 | tf_op jit(solution)/shard_map/dot_general | solution.py:71
  229.9 1.1 fusion.20
  231.0 4.1 %fusion.29 = f32[32,8,4096]{2,1,0:T(8,128)} fusion(bf16[768,4096,1]{1,0,2:T(8,128)(2,1)S(1)} %bitcast.69, s32[256]{0:T(256)S(1)} %copy-done.27, f32[256,768]{1,0:T(8,128)S(1)} %get-tuple-element.30, pred[256,768]{1,0:T(8,128)(4,1)S(1)} %fusion, f32[256]{0:T(256)S(1)} %get-tuple-element.3, pred[768]{0:T(1024)(128)(4,1)S(1)} %fusion.21), kind=kOutput, calls=%fused_computation.53 | convolution fusion | flops 1612382208 | bytes 11471616 | tf_op jit(solution)/shard_map/dot_general | solution.py:86
  235.2 1.2 copy.24
  236.3 3.6 %fusion.7 = f32[32,24,4096]{2,1,0:T(8,128)S(1)} fusion(bf16[32,24,256]{2,1,0:T(8,128)(2,1)S(1)} %bitcast.70, bf16[32,32,4096]{2,1,0:T(8,128)(2,1)} %bitcast.67), kind=kOutput, calls=%fused_computation.15 | convolution fusion | flops 1610612736 | bytes 15073280 | tf_op jit(solution)/shard_map/dot_general | solution.py:87
  243.9 3.6 %collective-permute-start.5 = (f32[256,128]{0,1:T(8,128)S(1)}, f32[256,128]{0,1:T(8,128)S(1)}, u32[]{:S(2)}, u32[]{:S(2)}) collective-permute-start(f32[256,128]{0,1:T(8,128)S(1)} %get-tuple-element.33), channel_id=1, source_target_pairs={{0,1},{1,0},{2,3},{3,2},{4,5},{5,4},{6,7},{7,6},{8,9},{9,8},{10,11... | collective-permute-start | bytes 393224 | tf_op jit(solution)/shard_map/ppermute | solution.py:17
  247.9 1.8 fusion.58
  249.8 1.6 collective-permute-done.5
  251.5 2.1 fusion.1
  254.9 85.3 %reduce-scatter.2.cloned.1.call-done = bf16[16,4096]{1,0:T(8,128)(2,1)} async-done(((bf16[256,4096]{1,0:T(8,128)(2,1)}), bf16[16,4096]{1,0:T(8,128)(2,1)}) %reduce-scatter.2.cloned.1.call-update) | async-done | bytes 131088 | tf_op jit(solution)/shard_map/reduce_scatter | solution.py:173
  341.4 2.0 fusion.2
  (129 shorter events, 16.2 us)
Async XLA Ops:
  7.2 71.7 %copy-start = (bf16[4096,128]{1,0:T(8,128)(2,1)S(1)}, bf16[4096,128]{1,0:T(8,128)(2,1)}, u32[]{:S(2)}) copy-start(bf16[4096,128]{1,0:T(8,128)(2,1)} %param.16) | copy-start | bytes 3145732
  7.2 68.8 %all-gather.3.cloned.1.call-start = ((), (), s32[]{:S(2)}) async-start(), calls=%async_computation.1 | async-start | bytes 2228224 | tf_op jit(solution)/shard_map/all_gather | solution.py:116
  10.6 211.8 %all-gather.5.cloned.1.call-start = ((), (), s32[]{:S(2)}) async-start(), calls=%async_computation.2 | async-start | bytes 8650752 | tf_op jit(solution)/shard_map/all_gather | solution.py:146
  10.6 27.7 %collective-permute-start = (bf16[4096,128]{1,0:T(8,128)(2,1)}, bf16[4096,128]{1,0:T(8,128)(2,1)S(1)}, u32[]{:S(2)}, u32[]{:S(2)}) collective-permute-start(bf16[4096,128]{1,0:T(8,128)(2,1)} %param.17), channel_id=1, source_target_pairs={{0,1},{1,0},{2,3},{3,2},{4,5},{5,4},{6,7},{7,6},{8,9},{9,8},{10,11... | collective-permute-start | bytes 3145736 | tf_op jit(solution)/shard_map/ppermute | solution.py:17
  15.7 63.6 %copy-start.20 = (s32[32]{0:T(128)}, s32[32]{0:T(128)S(1)}, u32[]{:S(2)}) copy-start(s32[32]{0:T(128)S(1)} %broadcast_add_fusion) | copy-start | bytes 388
  20.3 59.1 %copy-start.30 = (s32[16]{0:T(128)}, s32[16]{0:T(128)S(1)}, u32[]{:S(2)}) copy-start(s32[16]{0:T(128)S(1)} %iota_add_fusion) | copy-start | bytes 196
  20.4 58.9 %copy-start.23 = (f32[128]{0:T(128)S(1)}, f32[128]{0:T(128)}, u32[]{:S(2)}) copy-start(f32[128]{0:T(128)} %param.18) | copy-start | bytes 1540
  78.8 3.8 %copy-start.25 = (f32[128]{0:T(128)S(1)}, f32[128]{0:T(128)}, u32[]{:S(2)}) copy-start(f32[128]{0:T(128)} %param.19) | copy-start | bytes 1540
  78.9 5.4 %copy-start.2 = (bf16[128,4096]{1,0:T(8,128)(2,1)S(1)}, bf16[128,4096]{1,0:T(8,128)(2,1)}, u32[]{:S(2)}) copy-start(bf16[128,4096]{1,0:T(8,128)(2,1)} %param.20) | copy-start | bytes 3145732
  79.3 4.9 %copy-start.14 = (f32[32]{0:T(128)}, f32[32]{0:T(128)S(1)}, u32[]{:S(2)}) copy-start(f32[32]{0:T(128)S(1)} %add_rsqrt_fusion.3) | copy-start | bytes 388
  84.3 57.9 %copy-start.5 = (f32[4096]{0:T(1024)S(1)}, f32[4096]{0:T(1024)}, u32[]{:S(2)}) copy-start(f32[4096]{0:T(1024)} %param.21) | copy-start | bytes 49156
  85.4 14.7 %collective-permute-start.1 = (f32[32,4096]{1,0:T(8,128)S(1)}, f32[32,4096]{1,0:T(8,128)S(1)}, u32[]{:S(2)}, u32[]{:S(2)}) collective-permute-start(f32[32,4096]{1,0:T(8,128)S(1)} %convolution_add_fusion.1), channel_id=1, source_target_pairs={{0,1},{1,0},{2,3},{3,2},{4,5},{5,4},{6,7},{7,6},{8,9},{9,8},{10,11... | collective-permute-start | bytes 1572872 | tf_op jit(solution)/shard_map/ppermute | solution.py:140
  100.2 15.3 %collective-permute-start.2 = (f32[32,4096]{1,0:T(8,128)S(1)}, f32[32,4096]{1,0:T(8,128)S(1)}, u32[]{:S(2)}, u32[]{:S(2)}) collective-permute-start(f32[32,4096]{1,0:T(8,128)S(1)} %add.174), channel_id=1, source_target_pairs={{0,2},{1,3},{2,0},{3,1},{4,6},{5,7},{6,4},{7,5},{8,10},{9,11},{10,... | collective-permute-start | bytes 1572872 | tf_op jit(solution)/shard_map/ppermute | solution.py:140
  115.6 12.9 %collective-permute-start.3 = (f32[32,4096]{1,0:T(8,128)S(1)}, f32[32,4096]{1,0:T(8,128)S(1)}, u32[]{:S(2)}, u32[]{:S(2)}) collective-permute-start(f32[32,4096]{1,0:T(8,128)S(1)} %add.175), channel_id=1, source_target_pairs={{0,4},{1,5},{2,6},{3,7},{4,0},{5,1},{6,2},{7,3},{8,12},{9,13},{10,... | collective-permute-start | bytes 1572872 | tf_op jit(solution)/shard_map/ppermute | solution.py:140
  128.5 13.5 %collective-permute-start.4 = (f32[32,4096]{1,0:T(8,128)S(1)}, f32[32,4096]{1,0:T(8,128)S(1)}, u32[]{:S(2)}, u32[]{:S(2)}) collective-permute-start(f32[32,4096]{1,0:T(8,128)S(1)} %add.176), channel_id=1, source_target_pairs={{0,8},{1,9},{2,10},{3,11},{4,12},{5,13},{6,14},{7,15},{8,0},{9,1},... | collective-permute-start | bytes 1572872 | tf_op jit(solution)/shard_map/ppermute | solution.py:140
  142.2 98.1 %copy-start.13 = (f32[32]{0:T(128)}, f32[32]{0:T(128)S(1)}, u32[]{:S(2)}) copy-start(f32[32]{0:T(128)S(1)} %add_rsqrt_fusion.2) | copy-start | bytes 388
  142.4 97.8 %copy-start.16 = (f32[32]{0:T(128)}, f32[32]{0:T(128)S(1)}, u32[]{:S(2)}) copy-start(f32[32]{0:T(128)S(1)} %add_rsqrt_fusion.1) | copy-start | bytes 388
  143.3 196.9 %reduce-scatter.2.cloned.1.call-start = ((), (), s32[]{:S(2)}) async-start(), calls=%async_computation.3 | async-start | bytes 2228224 | tf_op jit(solution)/shard_map/reduce_scatter | solution.py:173
  222.4 3.2 copy-start.27
  229.9 5.3 %copy-start.28 = (f32[256]{0:T(256)}, f32[256]{0:T(256)S(1)}, u32[]{:S(2)}) copy-start(f32[256]{0:T(256)S(1)} %get-tuple-element.3) | copy-start | bytes 3076
  236.3 3.6 %copy-start.3 = (f32[32,8,4096]{2,1,0:T(8,128)S(1)}, f32[32,8,4096]{2,1,0:T(8,128)}, u32[]{:S(2)}) copy-start(f32[32,8,4096]{2,1,0:T(8,128)} %fusion.29) | copy-start | bytes 12582916
  240.2 2.6 copy-start.15
  240.2 2.8 copy-start.10
  240.2 2.8 copy-start.26
  240.2 7.7 %copy-start.21 = (s32[32]{0:T(128)S(1)}, s32[32]{0:T(128)}, u32[]{:S(2)}) copy-start(s32[32]{0:T(128)} %copy-done.20) | copy-start | bytes 388
  242.0 9.4 %copy-start.1 = (bf16[4096,128]{1,0:T(8,128)(2,1)S(1)}, bf16[4096,128]{1,0:T(8,128)(2,1)}, u32[]{:S(2)}) copy-start(bf16[4096,128]{1,0:T(8,128)(2,1)} %param.17) | copy-start | bytes 3145732
  243.9 7.5 %collective-permute-start.5 = (f32[256,128]{0,1:T(8,128)S(1)}, f32[256,128]{0,1:T(8,128)S(1)}, u32[]{:S(2)}, u32[]{:S(2)}) collective-permute-start(f32[256,128]{0,1:T(8,128)S(1)} %get-tuple-element.33), channel_id=1, source_target_pairs={{0,1},{1,0},{2,3},{3,2},{4,5},{5,4},{6,7},{7,6},{8,9},{9,8},{10,11... | collective-permute-start | bytes 393224 | tf_op jit(solution)/shard_map/ppermute | solution.py:17
  251.4 88.8 %copy-start.4 = (bf16[16,4096]{1,0:T(8,128)(2,1)S(1)}, bf16[16,4096]{1,0:T(8,128)(2,1)}, u32[]{:S(2)}) copy-start(bf16[16,4096]{1,0:T(8,128)(2,1)} %param.11) | copy-start | bytes 393220
  251.4 88.8 %copy-start.8 = (f32[4096]{0:T(1024)S(1)}, f32[4096]{0:T(1024)}, u32[]{:S(2)}) copy-start(f32[4096]{0:T(1024)} %param.15) | copy-start | bytes 49156
  251.4 88.8 %copy-start.19 = (f32[16]{0:T(128)S(1)}, f32[16]{0:T(128)}, u32[]{:S(2)}) copy-start(f32[16]{0:T(128)} %copy-done.18) | copy-start | bytes 196
  251.4 89.9 %copy-start.22 = (s32[32]{0:T(128)S(1)}, s32[32]{0:T(128)}, u32[]{:S(2)}) copy-start(s32[32]{0:T(128)} %copy-done.20) | copy-start | bytes 388
  251.4 89.9 %copy-start.31 = (s32[16]{0:T(128)S(1)}, s32[16]{0:T(128)}, u32[]{:S(2)}) copy-start(s32[16]{0:T(128)} %copy-done.30) | copy-start | bytes 196
  (10 other events, 17.3 us)
Sparse Core Ops, SparseCore 0:
  11.6 64.3 all-gather.2
  143.4 78.9 all-gather.4
  253.7 86.4 reduce-scatter.1
